TPU v7x, 32 devices: a whole 2x2x4 slice. The times are simulated.
32 devices in a mesh: patch: 16 (over z, y, x), head: 2 (over core).
Axes of the slice: x: 2, y: 2, z: 4, core: 2. Of those that a mesh axis runs over, the one named last changes fastest.
Arguments:
- hidden: bfloat16 [2, 3072, 3072], P(None, 'patch', 'head'), may hold values from -6 to 6
- stale_kv: bfloat16 [2, 3072, 3072], P(None, 'patch', 'head'), may hold values from -8 to 8
- modulation: float32 [2, 2, 3072], replicated, may hold values from -3 to 3
- attn_gate: float32 [2, 3072], P(None, 'head'), may hold values from 0.5 to 2
- w_qkv: bfloat16 [3072, 3, 3072], P(None, None, 'head'), may hold values from -2 to 2
- w_out: bfloat16 [3072, 3072], P('head'), may hold values from -0.109375 to 0.109375
Outputs:
- updated: bfloat16 [2, 3072, 3072], P(None, 'patch', 'head')
All inputs are finite; a program needn't handle non-finite values.
Results may differ from a plain program's by a relative error of at most 0.019.
Values may be sent and summed in bfloat16 or wider, within the bound.
A program may use at most 192 MiB of HBM per device.

v0:
```python
import functools
import math

import jax
import jax.numpy as jnp
from jax import lax
from jax.experimental import pallas as pl
from jax.experimental.pallas import tpu as pltpu
from jax.sharding import PartitionSpec as P

HEAD_DIM = 128
SCALE = HEAD_DIM ** (-0.5) * math.log2(math.e)


def layer_norm(values_in):
    mean_value = jnp.mean(values_in, axis=-1, keepdims=True)
    centred = values_in - mean_value
    variance = jnp.mean(centred * centred, axis=-1, keepdims=True)
    return centred * lax.rsqrt(variance + 1e-06)


def attend_kernel(ring, slab, q_ref, k_ref, v_ref, kf_ref, vf_ref, o_ref, kbuf, vbuf):
    mine = lax.rem(lax.axis_index("patch"), ring)
    group = q_ref.shape[0] // slab
    kbuf[...] = k_ref[:, 0]
    vbuf[...] = v_ref[:, 0]

    def one_slab(j, carry):
        rows = pl.ds(pl.multiple_of(j * slab, slab), slab)
        here = pl.ds(mine, 1)
        kbuf[here, rows] = kf_ref[rows][None]
        vbuf[here, rows] = vf_ref[rows][None]
        keys = kbuf[...].reshape(ring * group * slab, HEAD_DIM)
        values = vbuf[...].reshape(ring * group * slab, HEAD_DIM)
        scores = lax.dot_general(
            q_ref[rows], keys, (((1,), (1,)), ((), ())), preferred_element_type=jnp.float32
        )
        peak = jnp.max(scores, axis=-1, keepdims=True)
        weights = jnp.exp2((scores - peak) * SCALE)
        total = jnp.sum(weights, axis=-1, keepdims=True)
        summed = jnp.dot(weights.astype(jnp.bfloat16), values, preferred_element_type=jnp.float32)
        o_ref[rows] = (summed / total).astype(jnp.bfloat16)
        kbuf[here, rows] = k_ref[here, 0, rows]
        vbuf[here, rows] = v_ref[here, 0, rows]
        return carry

    lax.fori_loop(0, group, one_slab, 0)


def attend(ring, slab, queries, gathered, fresh_keys, fresh_values):
    rows, width = queries.shape
    heads = width // HEAD_DIM
    flat = pl.BlockSpec((rows, HEAD_DIM), lambda h: (0, h))
    return pl.pallas_call(
        functools.partial(attend_kernel, ring, slab),
        grid=(heads,),
        out_shape=jax.ShapeDtypeStruct((rows, width), jnp.bfloat16),
        in_specs=[
            flat,
            pl.BlockSpec((ring, 1, rows, HEAD_DIM), lambda h: (0, 0, 0, h)),
            pl.BlockSpec((ring, 1, rows, HEAD_DIM), lambda h: (0, 1, 0, h)),
            flat,
            flat,
        ],
        out_specs=flat,
        scratch_shapes=[
            pltpu.VMEM((ring, rows, HEAD_DIM), jnp.bfloat16),
            pltpu.VMEM((ring, rows, HEAD_DIM), jnp.bfloat16),
        ],
        compiler_params=pltpu.CompilerParams(vmem_limit_bytes=48 * 2**20),
        cost_estimate=pl.CostEstimate(
            flops=4 * rows * width * rows * ring,
            bytes_accessed=2 * width * rows * (2 * ring + 4),
            transcendentals=rows * rows * ring * heads,
        ),
    )(queries, gathered, gathered, fresh_keys, fresh_values)


K0, V0, Q0, Q1, K1, V1, SK, SV = range(8)
PLACE = {K0: (1, 0), V0: (2, 0), Q0: (0, 0), Q1: (0, 1), K1: (1, 1), V1: (2, 1)}
PLANE = {SK: 0, SV: 1, K0: 2, V0: 3}
TILE = 256
MESH = pl.DeviceIdType.MESH


def attend_step(query, fresh_k, fresh_v, own, others, kbuf, vbuf, store):
    group, slab, _ = kbuf.shape
    kbuf[...], vbuf[...] = own()

    def one_slot(j, carry):
        here = pl.ds(j, 1)
        kept_k, kept_v = kbuf[here], vbuf[here]
        kbuf[here] = fresh_k(here)
        vbuf[here] = fresh_v(here)
        rows = query(here).reshape(slab, HEAD_DIM)
        blocks = [(kbuf[...], vbuf[...])] + [other() for other in others]
        blocks = [[part.reshape(group * slab, HEAD_DIM) for part in block] for block in blocks]
        scores = [
            lax.dot_general(rows, k, (((1,), (1,)), ((), ())), preferred_element_type=jnp.float32)
            for k, _ in blocks
        ]
        peak = functools.reduce(
            jnp.maximum, [jnp.max(block, axis=-1, keepdims=True) for block in scores]
        )
        total, summed = 0.0, 0.0
        for block, (_, v) in zip(scores, blocks):
            weights = jnp.exp2((block - peak) * SCALE)
            total += jnp.sum(weights, axis=-1, keepdims=True)
            summed += jnp.dot(weights.astype(jnp.bfloat16), v, preferred_element_type=jnp.float32)
        store(here, (summed / total).astype(jnp.bfloat16)[None])
        kbuf[here] = kept_k
        vbuf[here] = kept_v
        return carry

    lax.fori_loop(0, group, one_slot, 0)


def block_kernel(
    ring, hidden_ref, stale_ref, mod_ref, gate_ref, w_qkv_ref, w_out_ref, updated_ref,
    hid, normed, w_buf, proj, col, gath, out, att, w_out, give, take, kbuf, vbuf,
    z_send, z_recv, loc_sem, f_send, f_recv, o_send, o_recv, w_sem, w_out_sem, hid_sem, p_send, p_recv,
):
    me, core = lax.axis_index("patch"), lax.axis_index("head")
    z, p = lax.div(me, ring), lax.rem(me, ring)
    _, group, slab, part = col.shape
    _, steps, _, width = hid.shape
    heads = part // HEAD_DIM

    def column_peer(d):
        return {"patch": lax.rem(z + d + group, group) * ring + p}

    beside = {"patch": z * ring + p + 1 - 2 * lax.rem(p, 2)}
    above = {"patch": z * ring + lax.rem(p + 2, 4)}
    twin = {"head": 1 - core}
    barrier = pltpu.get_barrier_semaphore()
    greeted = [column_peer(d) for d in range(1, group)] + [beside, above]
    for peer in greeted + [twin]:
        pl.semaphore_signal(barrier, inc=1, device_id=peer, device_id_type=MESH)

    def weight_copy(n):
        which, half = (1, 2, 0)[n // 2], n % 2
        columns = pl.ds(half * (width // 2), width // 2)
        return pltpu.make_async_copy(
            w_qkv_ref.at[which, :, columns], w_buf.at[n % 2], w_sem.at[n % 2]
        )

    weight_copy(0).start()
    weight_copy(1).start()
    hid_own = pltpu.make_async_copy(hidden_ref, hid.at[core], hid_sem.at[0])
    hid_own.start()
    pl.semaphore_wait(barrier, group + 2)
    hid_swap = pltpu.make_async_remote_copy(
        src_ref=hidden_ref, dst_ref=hid.at[core], send_sem=hid_sem.at[1], recv_sem=hid_sem.at[2],
        device_id=twin, device_id_type=MESH,
    )
    hid_swap.start()

    def source(a, owner):
        columns = pl.ds(pl.multiple_of(owner * part, part), part)
        if a in (SK, SV):
            return stale_ref.at[a - SK, :, columns]
        which, step = PLACE[a]
        return proj.at[which, pl.ds(step * slab, slab), columns]

    moves = {}

    def spread(arrays):
        for a in arrays:
            moves[a, 0] = pltpu.make_async_copy(source(a, z), col.at[a, 0], loc_sem.at[a])
            moves[a, 0].start()
        for d in range(1, group):
            for a in arrays:
                moves[a, d] = pltpu.make_async_remote_copy(
                    src_ref=source(a, lax.rem(z + d, group)),
                    dst_ref=col.at[a, d],
                    send_sem=z_send.at[a, d],
                    recv_sem=z_recv.at[a, d],
                    device_id=column_peer(d),
                    device_id_type=MESH,
                )
                moves[a, d].start()

    def arrive(a, d):
        if d == 0:
            moves[a, 0].wait()
        else:
            moves[a, d].wait_recv()

    forwards = {}

    def send_plane(a, d, e, src, peer):
        slot = PLANE[a]
        forwards[a, d, e] = pltpu.make_async_remote_copy(
            src_ref=src,
            dst_ref=gath.at[slot, e, d],
            send_sem=f_send.at[slot, d, e],
            recv_sem=f_recv.at[slot, d, e],
            device_id=peer,
            device_id_type=MESH,
        )
        forwards[a, d, e].start()

    def forward(pair, d):
        for a in pair:
            arrive(a, d)
            send_plane(a, d, 0, col.at[a, d], beside)
            send_plane(a, d, 1, col.at[a, d], above)

    def relay(pair, d):
        for a, e, peer in ((pair[0], 1, beside), (pair[1], 0, above)):
            forwards[a, d, e].wait_recv()
            relayed.add((a, d, e))
            send_plane(a, d, 2, gath.at[PLANE[a], e, d], peer)

    relayed = set()
    stale, past = (SK, SV), (K0, V0)
    spread((SK, SV))
    forward(stale, 0)
    hid_own.wait()
    hid_swap.wait_recv()

    block = slab // 4

    def norm_rows(n, carry):
        step = lax.div(n, 4)
        rows = pl.ds(pl.multiple_of(lax.rem(n, 4) * block, block), block)
        here = pl.ds(step, 1)
        halves = [hid[c, here, rows].reshape(block, width).astype(jnp.float32) for c in range(2)]
        count = 2 * width
        mean_value = sum(jnp.sum(half, axis=-1, keepdims=True) for half in halves) / count
        centred = [half - mean_value for half in halves]
        variance = sum(jnp.sum(half * half, axis=-1, keepdims=True) for half in centred) / count
        inverse = lax.rsqrt(variance + 1e-06)
        landing = pl.ds(pl.multiple_of(n * block, block), block)
        for c in range(2):
            lanes = pl.ds(c * width, width)
            shift = mod_ref[here, 0, lanes].reshape(1, width)
            scale = mod_ref[here, 1, lanes].reshape(1, width)
            value = centred[c] * inverse * (1.0 + scale) + shift
            normed[landing, lanes] = value.astype(jnp.bfloat16)
        return carry

    lax.fori_loop(0, 4 * steps, norm_rows, 0)

    def project(n):
        which, half = (1, 2, 0)[n // 2], n % 2
        weight_copy(n).wait()

        def tile(t, carry):
            lanes = pl.ds(pl.multiple_of(t * TILE, TILE), TILE)
            landing = pl.ds(pl.multiple_of(half * (width // 2) + t * TILE, TILE), TILE)
            value = jnp.dot(normed[...], w_buf[n % 2, :, lanes], preferred_element_type=jnp.float32)
            proj[which, :, landing] = value.astype(jnp.bfloat16)
            return carry

        lax.fori_loop(0, width // 2 // TILE, tile, 0)
        if n + 2 < 6:
            weight_copy(n + 2).start()

    project(0)
    project(1)
    spread((K0,))
    forward(stale, 1)
    relay(stale, 0)
    project(2)
    project(3)
    spread((V0,))
    forward(stale, 2)
    relay(stale, 1)
    project(4)
    project(5)
    spread((Q0,))
    spread((Q1,))
    spread((K1, V1))
    w_out_copies = []
    for side in range(2):
        half = 1 - core if side == 0 else core
        columns = pl.ds(pl.multiple_of(half * width, width), width)
        w_out_copies.append(
            pltpu.make_async_copy(w_out_ref.at[:, columns], w_out.at[side], w_out_sem.at[side])
        )
        w_out_copies[side].start()
    forward(stale, 3)
    relay(stale, 2)
    forward(past, 0)
    relay(stale, 3)
    forward(past, 1)
    relay(past, 0)
    forward(past, 2)
    relay(past, 1)
    forward(past, 3)

    returns = {}

    def run_step(step, query_a, key_a, value_a, past_k, past_v, between):
        for h in range(heads):
            lanes = pl.ds(h * HEAD_DIM, HEAD_DIM)

            def store(here, value):
                out[step, h, here] = value

            attend_step(
                lambda here: col[query_a, here, :, lanes],
                lambda here: col[key_a, here, :, lanes],
                lambda here: col[value_a, here, :, lanes],
                lambda: (col[past_k, :, :, lanes], col[past_v, :, :, lanes]),
                [
                    lambda e=e: (
                        gath[PLANE[past_k], e, :, :, lanes],
                        gath[PLANE[past_v], e, :, :, lanes],
                    )
                    for e in range(3)
                ],
                kbuf, vbuf, store,
            )
            columns = pl.ds(pl.multiple_of(z * part + h * HEAD_DIM, HEAD_DIM), HEAD_DIM)
            landing = att.at[step, :, columns]
            for j in range(group):
                if j == 0:
                    back = pltpu.make_async_copy(out.at[step, h, 0], landing, o_recv.at[step, h, 0])
                else:
                    back = pltpu.make_async_remote_copy(
                        src_ref=out.at[step, h, j],
                        dst_ref=landing,
                        send_sem=o_send.at[step, h, j],
                        recv_sem=o_recv.at[step, h, j],
                        device_id=column_peer(-j),
                        device_id_type=MESH,
                    )
                back.start()
                returns[step, h, j] = back
            between(h)

    def wait_plane(arrays):
        for key, copy in forwards.items():
            if key[0] in arrays and key not in relayed:
                copy.wait_recv()

    def branch_tile(step, side, t):
        lanes = pl.ds(pl.multiple_of(t * TILE, TILE), TILE)
        return lanes, jnp.dot(att[step], w_out[side, :, lanes], preferred_element_type=jnp.float32)

    def share(step):
        for back in [copy for key, copy in returns.items() if key[0] == step]:
            back.wait()

        def tile(t, carry):
            lanes, value = branch_tile(step, 0, t)
            give[step, :, lanes] = value.astype(jnp.bfloat16)
            return carry

        lax.fori_loop(0, width // TILE, tile, 0)
        copy = pltpu.make_async_remote_copy(
            src_ref=give.at[step], dst_ref=take.at[step],
            send_sem=p_send.at[step], recv_sem=p_recv.at[step],
            device_id=twin, device_id_type=MESH,
        )
        copy.start()
        return copy

    def update(step, copy):
        copy.wait_recv()

        def tile(t, carry):
            lanes, value = branch_tile(step, 1, t)
            value = value + take[step, :, lanes].astype(jnp.float32)
            before = hid[pl.ds(core, 1), step, :, lanes].reshape(slab, TILE).astype(jnp.float32)
            after = before + gate_ref[pl.ds(step, 1), lanes] * value
            updated_ref[step, :, lanes] = after.astype(jnp.bfloat16)
            return carry

        lax.fori_loop(0, width // TILE, tile, 0)

    for d in range(group):
        arrive(Q0, d)
    wait_plane((SK, SV))
    run_step(0, Q0, K0, V0, SK, SV, lambda h: relay(past, h + 2) if h < 2 else None)
    for a in (Q1, K1, V1):
        for d in range(group):
            arrive(a, d)
    wait_plane((K0, V0))
    run_step(1, Q1, K1, V1, K0, V0, lambda h: None)
    for copy in w_out_copies:
        copy.wait()
    shares = [share(step) for step in range(steps)]
    for step in range(steps):
        update(step, shares[step])
    for copy in shares + [hid_swap] + list(forwards.values()):
        copy.wait_send()
    for (_, d), copy in moves.items():
        if d > 0:
            copy.wait_send()


def whole_block(group, ring, hidden, stale_kv, modulation, attn_gate, w_qkv, w_out):
    steps, slab, width = hidden.shape
    part = width // group
    heads = part // HEAD_DIM
    bf16, dma = jnp.bfloat16, pltpu.SemaphoreType.DMA
    vmem, anywhere = pl.BlockSpec(memory_space=pltpu.VMEM), pl.BlockSpec(memory_space=pl.ANY)
    return pl.pallas_call(
        functools.partial(block_kernel, ring),
        out_shape=jax.ShapeDtypeStruct(hidden.shape, bf16),
        in_specs=[anywhere, anywhere, vmem, vmem, anywhere, anywhere],
        out_specs=vmem,
        scratch_shapes=[
            pltpu.VMEM((2, steps, slab, width), bf16),
            pltpu.VMEM((steps * slab, 2 * width), bf16),
            pltpu.VMEM((2, 2 * width, width // 2), bf16),
            pltpu.VMEM((3, steps * slab, width), bf16),
            pltpu.VMEM((8, group, slab, part), bf16),
            pltpu.VMEM((4, 3, group, slab, part), bf16),
            pltpu.VMEM((steps, heads, group, slab, HEAD_DIM), bf16),
            pltpu.VMEM((steps, slab, width), bf16),
            pltpu.VMEM((2, width, width), bf16),
            pltpu.VMEM((steps, slab, width), bf16),
            pltpu.VMEM((steps, slab, width), bf16),
            pltpu.VMEM((group, slab, HEAD_DIM), bf16),
            pltpu.VMEM((group, slab, HEAD_DIM), bf16),
            dma((8, group)),
            dma((8, group)),
            dma((8,)),
            dma((4, group, 3)),
            dma((4, group, 3)),
            dma((steps, heads, group)),
            dma((steps, heads, group)),
            dma((2,)),
            dma((2,)),
            dma((3,)),
            dma((steps,)),
            dma((steps,)),
        ],
        compiler_params=pltpu.CompilerParams(
            collective_id=0, has_side_effects=True, vmem_limit_bytes=60 * 2**20
        ),
        cost_estimate=pl.CostEstimate(
            flops=steps * slab * width * (16 * width + 4 * slab * group * ring),
            bytes_accessed=2 * width * (8 * width + 6 * steps * slab),
            transcendentals=steps * slab * slab * group * ring * width // HEAD_DIM,
        ),
    )(hidden, stale_kv, modulation, attn_gate, jnp.transpose(w_qkv, (1, 0, 2)), w_out)


def finish(outs, hidden, attn_gate, w_out):
    partial_out = jnp.dot(outs, w_out, preferred_element_type=jnp.float32)
    branch = lax.psum_scatter(
        partial_out.astype(jnp.bfloat16), "head", scatter_dimension=1, tiled=True
    ).astype(jnp.float32)
    gated = attn_gate[:, None] * branch.reshape(hidden.shape)
    return (hidden.astype(jnp.float32) + gated).astype(jnp.bfloat16)


def on_device(patches, hidden, stale_kv, modulation, attn_gate, w_qkv, w_out):
    steps, slab, width = hidden.shape
    group = math.gcd(width // HEAD_DIM, patches)
    ring = patches // group
    if group == 4 and ring == 4 and steps == 2 and w_out.shape[1] == 2 * width:
        return whole_block(group, ring, hidden, stale_kv, modulation, attn_gate, w_qkv, w_out)
    columns = [[g * ring + p for g in range(group)] for p in range(ring)]
    planes = [[g * ring + p for p in range(ring)] for g in range(group)]
    part = width // group

    def spread(rows):
        n = rows.shape[0]
        if group == 1:
            return rows
        split = rows.reshape(n, slab, group, part).transpose(2, 0, 1, 3)
        got = lax.all_to_all(split, "patch", 0, 0, axis_index_groups=columns, tiled=True)
        return got.transpose(1, 0, 2, 3).reshape(n, group * slab, part)

    def gather(rows):
        return lax.all_gather(rows, "patch", axis=0, axis_index_groups=planes)

    stale_all = gather(spread(stale_kv))
    full_rows = lax.all_gather(hidden, "head", axis=2, tiled=True)
    normed = layer_norm(full_rows.astype(jnp.float32))
    normed = (normed * (1.0 + modulation[:, 1][:, None]) + modulation[:, 0][:, None]).astype(
        jnp.bfloat16
    )
    projected = jnp.dot(
        normed.reshape(steps * slab, -1),
        w_qkv.reshape(w_qkv.shape[0], -1),
        preferred_element_type=jnp.float32,
    ).astype(jnp.bfloat16)
    projected = projected.reshape(steps, slab, 3, width).transpose(0, 2, 1, 3)
    q0, k0, v0, q1, k1, v1 = spread(projected.reshape(steps * 3, slab, width))
    fresh_all = gather(jnp.stack([k0, v0]))
    outs = jnp.stack(
        [attend(ring, slab, q0, stale_all, k0, v0), attend(ring, slab, q1, fresh_all, k1, v1)]
    )
    if group > 1:
        back = outs.reshape(steps, group, slab, part).transpose(1, 0, 2, 3)
        back = lax.all_to_all(back, "patch", 0, 0, axis_index_groups=columns, tiled=True)
        outs = back.transpose(1, 2, 0, 3).reshape(steps, slab, width)
    return finish(outs.reshape(steps * slab, width), hidden, attn_gate, w_out)


def solution(mesh):
    in_specs = (
        P(None, "patch", "head"),
        P(None, "patch", "head"),
        P(),
        P(None, "head"),
        P(None, None, "head"),
        P("head", None),
    )
    return jax.shard_map(
        functools.partial(on_device, mesh.shape["patch"]),
        mesh=mesh,
        in_specs=in_specs,
        out_specs=P(None, "patch", "head"),
        check_vma=False,
    )
```

profile of v0, /device:TPU:0, one launch (start us, length us, event | category | flops | bytes accessed | tf_op | source)
XLA Modules:
  0.0 150.7 jit_solution(5743347791431737459)
XLA Ops:
  0.0 148.4 %shard_map.64 = bf16[2,192,1536]{2,1,0:T(8,128)(2,1)} custom-call(bf16[2,192,1536]{2,1,0:T(8,128)(2,1)} %hidden_ref.1, bf16[2,192,1536]{2,1,0:T(8,128)(2,1)} %stale_ref.1, f32[2,2,3072]{2,1,0:T(2,128)} %mod_ref.1, f32[2,1536]{1,0:T(2,128)} %gate_ref.1, bf16[3,3072,1536]{2,1,0:T(8,128)(2,1)} %bitcast.1, bf16[1536,3072]{1,0:T(8,128)(2,1)} %w_out_ref.1), custom_call_target="tpu_custom_call" | custom-call | flops 21743271936 | bytes 44826624 | tf_op jit(solution)/shard_map/pallas_call | solution.py:401
  148.4 2.4 %copy.8 = bf16[2,192,1536]{2,1,0:T(8,128)(2,1)} copy(bf16[2,192,1536]{2,1,0:T(8,128)(2,1)} %shard_map.64) | data formatting | bytes 2359296
where the time goes:
time: 151 us
  Pallas kernels  148 us (98%)
  local copies, waits for them, and re-layouts  2.36 us (2%)
    pallas_call x1, Pallas kernels, whole_block(): pl.pallas_call(functools.partial(block_kernel, ring), out_shape=jax.Shape...  148 us

commit v1 on v0

--- a/solution.py
+++ b/solution.py
@@ -76,8 +76,8 @@
     )(queries, gathered, gathered, fresh_keys, fresh_values)
 
 
-K0, V0, Q0, Q1, K1, V1, SK, SV = range(8)
-PLACE = {K0: (1, 0), V0: (2, 0), Q0: (0, 0), Q1: (0, 1), K1: (1, 1), V1: (2, 1)}
+K0, V0, Q0, Q1, SK, SV = range(6)
+PLACE = {K0: (1, 0), V0: (2, 0), Q0: (0, 0), Q1: (0, 1)}
 PLANE = {SK: 0, SV: 1, K0: 2, V0: 3}
 TILE = 256
 MESH = pl.DeviceIdType.MESH
@@ -115,10 +115,28 @@
     lax.fori_loop(0, group, one_slot, 0)
 
 
+def weigh(rows, blocks):
+    scores = [
+        lax.dot_general(rows, k, (((1,), (1,)), ((), ())), preferred_element_type=jnp.float32)
+        for k, _ in blocks
+    ]
+    peak = functools.reduce(
+        jnp.maximum, [jnp.max(block, axis=-1, keepdims=True) for block in scores]
+    )
+    total, summed = 0.0, 0.0
+    for block, (_, v) in zip(scores, blocks):
+        weights = jnp.exp2((block - peak) * SCALE)
+        total += jnp.sum(weights, axis=-1, keepdims=True)
+        summed += jnp.dot(weights.astype(jnp.bfloat16), v, preferred_element_type=jnp.float32)
+    return summed / total, peak * SCALE + jnp.log2(total)
+
+
 def block_kernel(
     ring, hidden_ref, stale_ref, mod_ref, gate_ref, w_qkv_ref, w_out_ref, updated_ref,
     hid, normed, w_buf, proj, col, gath, out, att, w_out, give, take, kbuf, vbuf,
+    near, near_level, level, level_out, level_in,
     z_send, z_recv, loc_sem, f_send, f_recv, o_send, o_recv, w_sem, w_out_sem, hid_sem, p_send, p_recv,
+    l_send, l_recv,
 ):
     me, core = lax.axis_index("patch"), lax.axis_index("head")
     z, p = lax.div(me, ring), lax.rem(me, ring)
@@ -271,7 +289,6 @@
     project(5)
     spread((Q0,))
     spread((Q1,))
-    spread((K1, V1))
     w_out_copies = []
     for side in range(2):
         half = 1 - core if side == 0 else core
@@ -290,7 +307,77 @@
     relay(past, 1)
     forward(past, 3)
 
+    def attend_near(h, carry):
+        lanes = pl.ds(pl.multiple_of(h * HEAD_DIM, HEAD_DIM), HEAD_DIM)
+        rows = pl.ds(slab, slab)
+        value, weight = weigh(proj[0, rows, lanes], [(proj[1, rows, lanes], proj[2, rows, lanes])])
+        near[pl.ds(h, 1)] = value[None]
+        near_level[pl.ds(h, 1)] = jnp.broadcast_to(weight, (slab, HEAD_DIM))[None]
+        return carry
+
+    lax.fori_loop(0, width // HEAD_DIM, attend_near, 0)
+    level[...] = jnp.zeros_like(level)
+
     returns = {}
+
+    def attend_far(h, lanes, e_slots):
+        def one_slot(j, carry):
+            def block(ref, a):
+                rest = [ref[a, pl.ds(lax.rem(j + i, group), 1), :, lanes] for i in range(1, group)]
+                return jnp.concatenate(rest, axis=0).reshape((group - 1) * slab, HEAD_DIM)
+
+            blocks = [(block(col, K0), block(col, V0))]
+            for e in e_slots:
+                blocks.append(
+                    tuple(
+                        gath[PLANE[a], e, :, :, lanes].reshape(group * slab, HEAD_DIM)
+                        for a in (K0, V0)
+                    )
+                )
+            here = pl.ds(j, 1)
+            value, weight = weigh(col[Q1, here, :, lanes].reshape(slab, HEAD_DIM), blocks)
+            out[1, h, here] = value.astype(jnp.bfloat16)[None]
+            places = lax.broadcasted_iota(jnp.int32, (slab, HEAD_DIM), 1)
+            held = level[here, 0:slab].reshape(slab, HEAD_DIM)
+            level[here, 0:slab] = jnp.where(places == h, weight, held)[None]
+            return carry
+
+        lax.fori_loop(0, group, one_slot, 0)
+
+    levels = []
+
+    def send_levels():
+        for j in range(group):
+            level_out[j] = jnp.transpose(level[j])[:8]
+        for j in range(group):
+            if j == 0:
+                copy = pltpu.make_async_copy(level_out.at[0], level_in.at[z], l_recv.at[0])
+            else:
+                copy = pltpu.make_async_remote_copy(
+                    src_ref=level_out.at[j], dst_ref=level_in.at[z],
+                    send_sem=l_send.at[j], recv_sem=l_recv.at[j],
+                    device_id=column_peer(-j), device_id_type=MESH,
+                )
+            copy.start()
+            levels.append(copy)
+
+    def merge():
+        for back in [copy for key, copy in returns.items() if key[0] == 1] + levels:
+            back.wait()
+        for u in range(group):
+            padded = jnp.concatenate(
+                [level_in[u], jnp.zeros((HEAD_DIM - 8, level_in.shape[2]), jnp.float32)], axis=0
+            )
+            columns = jnp.transpose(padded)
+            for h in range(heads):
+                lanes = pl.ds(u * part + h * HEAD_DIM, HEAD_DIM)
+                far_level = columns[:slab, h : h + 1]
+                here_level = near_level[u * heads + h][:, :1]
+                top = jnp.maximum(far_level, here_level)
+                far_share, near_share = jnp.exp2(far_level - top), jnp.exp2(here_level - top)
+                value = att[1, :, lanes].astype(jnp.float32) * far_share
+                value = value + near[u * heads + h] * near_share
+                att[1, :, lanes] = (value / (far_share + near_share)).astype(jnp.bfloat16)
 
     def run_step(step, query_a, key_a, value_a, past_k, past_v, between):
         for h in range(heads):
@@ -299,20 +386,23 @@
             def store(here, value):
                 out[step, h, here] = value
 
-            attend_step(
-                lambda here: col[query_a, here, :, lanes],
-                lambda here: col[key_a, here, :, lanes],
-                lambda here: col[value_a, here, :, lanes],
-                lambda: (col[past_k, :, :, lanes], col[past_v, :, :, lanes]),
-                [
-                    lambda e=e: (
-                        gath[PLANE[past_k], e, :, :, lanes],
-                        gath[PLANE[past_v], e, :, :, lanes],
-                    )
-                    for e in range(3)
-                ],
-                kbuf, vbuf, store,
-            )
+            if step == 0:
+                attend_step(
+                    lambda here: col[query_a, here, :, lanes],
+                    lambda here: col[key_a, here, :, lanes],
+                    lambda here: col[value_a, here, :, lanes],
+                    lambda: (col[past_k, :, :, lanes], col[past_v, :, :, lanes]),
+                    [
+                        lambda e=e: (
+                            gath[PLANE[past_k], e, :, :, lanes],
+                            gath[PLANE[past_v], e, :, :, lanes],
+                        )
+                        for e in range(3)
+                    ],
+                    kbuf, vbuf, store,
+                )
+            else:
+                attend_far(h, lanes, range(3))
             columns = pl.ds(pl.multiple_of(z * part + h * HEAD_DIM, HEAD_DIM), HEAD_DIM)
             landing = att.at[step, :, columns]
             for j in range(group):
@@ -341,8 +431,11 @@
         return lanes, jnp.dot(att[step], w_out[side, :, lanes], preferred_element_type=jnp.float32)
 
     def share(step):
-        for back in [copy for key, copy in returns.items() if key[0] == step]:
-            back.wait()
+        if step == 1:
+            merge()
+        else:
+            for back in [copy for key, copy in returns.items() if key[0] == 0]:
+                back.wait()
 
         def tile(t, carry):
             lanes, value = branch_tile(step, 0, t)
@@ -375,11 +468,11 @@
         arrive(Q0, d)
     wait_plane((SK, SV))
     run_step(0, Q0, K0, V0, SK, SV, lambda h: relay(past, h + 2) if h < 2 else None)
-    for a in (Q1, K1, V1):
-        for d in range(group):
-            arrive(a, d)
+    for d in range(group):
+        arrive(Q1, d)
     wait_plane((K0, V0))
-    run_step(1, Q1, K1, V1, K0, V0, lambda h: None)
+    run_step(1, Q1, K0, V0, K0, V0, lambda h: None)
+    send_levels()
     for copy in w_out_copies:
         copy.wait()
     shares = [share(step) for step in range(steps)]
@@ -408,7 +501,7 @@
             pltpu.VMEM((steps * slab, 2 * width), bf16),
             pltpu.VMEM((2, 2 * width, width // 2), bf16),
             pltpu.VMEM((3, steps * slab, width), bf16),
-            pltpu.VMEM((8, group, slab, part), bf16),
+            pltpu.VMEM((6, group, slab, part), bf16),
             pltpu.VMEM((4, 3, group, slab, part), bf16),
             pltpu.VMEM((steps, heads, group, slab, HEAD_DIM), bf16),
             pltpu.VMEM((steps, slab, width), bf16),
@@ -417,9 +510,14 @@
             pltpu.VMEM((steps, slab, width), bf16),
             pltpu.VMEM((group, slab, HEAD_DIM), bf16),
             pltpu.VMEM((group, slab, HEAD_DIM), bf16),
-            dma((8, group)),
-            dma((8, group)),
-            dma((8,)),
+            pltpu.VMEM((width // HEAD_DIM, slab, HEAD_DIM), jnp.float32),
+            pltpu.VMEM((width // HEAD_DIM, slab, HEAD_DIM), jnp.float32),
+            pltpu.VMEM((group, 256, HEAD_DIM), jnp.float32),
+            pltpu.VMEM((group, 8, 256), jnp.float32),
+            pltpu.VMEM((group, 8, 256), jnp.float32),
+            dma((6, group)),
+            dma((6, group)),
+            dma((6,)),
             dma((4, group, 3)),
             dma((4, group, 3)),
             dma((steps, heads, group)),
@@ -429,6 +527,8 @@
             dma((3,)),
             dma((steps,)),
             dma((steps,)),
+            dma((group,)),
+            dma((group,)),
         ],
         compiler_params=pltpu.CompilerParams(
             collective_id=0, has_side_effects=True, vmem_limit_bytes=60 * 2**20
@@ -454,7 +554,7 @@
     steps, slab, width = hidden.shape
     group = math.gcd(width // HEAD_DIM, patches)
     ring = patches // group
-    if group == 4 and ring == 4 and steps == 2 and w_out.shape[1] == 2 * width:
+    if group == 4 and ring == 4 and steps == 2 and slab <= 256 and w_out.shape[1] == 2 * width:
         return whole_block(group, ring, hidden, stale_kv, modulation, attn_gate, w_qkv, w_out)
     columns = [[g * ring + p for g in range(group)] for p in range(ring)]
     planes = [[g * ring + p for p in range(ring)] for g in range(group)]

time: 151 us -> 135 us (0.89)
  Pallas kernels: 148 us -> 132 us
    pallas_call x1, Pallas kernels: 148 us -> 132 us  [whole_block(): pl.pallas_call(functools.partial(block_kernel, ring), out_shape=jax.Shape...]
where the time goes in v1:
time: 135 us
  Pallas kernels  132 us (98%)
  local copies, waits for them, and re-layouts  2.36 us (2%)
    pallas_call x1, Pallas kernels, whole_block(): pl.pallas_call(functools.partial(block_kernel, ring), out_shape=jax.Shape...  132 us

profile of v1, /device:TPU:0, one launch (start us, length us, event | category | flops | bytes accessed | tf_op | source)
XLA Modules:
  0.0 134.8 jit_solution(3470672534229357894)
XLA Ops:
  0.0 132.4 %shard_map.64 = bf16[2,192,1536]{2,1,0:T(8,128)(2,1)} custom-call(bf16[2,192,1536]{2,1,0:T(8,128)(2,1)} %hidden_ref.1, bf16[2,192,1536]{2,1,0:T(8,128)(2,1)} %stale_ref.1, f32[2,2,3072]{2,1,0:T(2,128)} %mod_ref.1, f32[2,1536]{1,0:T(2,128)} %gate_ref.1, bf16[3,3072,1536]{2,1,0:T(8,128)(2,1)} %bitcast.1, bf16[1536,3072]{1,0:T(8,128)(2,1)} %w_out_ref.1), custom_call_target="tpu_custom_call" | custom-call | flops 21743271936 | bytes 44826624 | tf_op jit(solution)/shard_map/pallas_call | solution.py:494
  132.4 2.4 %copy.8 = bf16[2,192,1536]{2,1,0:T(8,128)(2,1)} copy(bf16[2,192,1536]{2,1,0:T(8,128)(2,1)} %shard_map.64) | data formatting | bytes 2359296
